TPU v7x, 32 devices: a whole 2x2x4 slice. The times are simulated.
32 devices in a mesh: ens: 2 (over y), tm: 4 (over z), space: 4 (over x, core).
Axes of the slice: x: 2, y: 2, z: 4, core: 2. Of those that a mesh axis runs over, the one named last changes fastest.
Arguments:
- initial: float32 [512, 2048], P(('ens', 'space')), parts along dimension 0, may hold values from -6 to 6
- diffusivity: float32 [512, 2048], P(('ens', 'space')), parts along dimension 0, may hold values from 0.04 to 0.06
- velocity_x: float32 [512, 2048], P(('ens', 'space')), parts along dimension 0, may hold values from -0.08 to 0.08
- velocity_y: float32 [512, 2048], P(('ens', 'space')), parts along dimension 0, may hold values from -0.08 to 0.08
- source: float32 [512, 2048], P(('ens', 'space')), parts along dimension 0, may hold values from -0.3 to 0.3
Outputs:
- end_states: float32 [4, 512, 2048], P('tm', ('ens', 'space')), parts along dimension 1
There are 2 independent parts, one for each index of `ens`. A program takes and returns all parts, laid end to end along the dimension named above; each array names one. Nothing has to cross between parts.
All inputs are finite; a program needn't handle non-finite values.
Results may differ from a plain program's by a relative error of at most 0.0045.
Values may be sent and summed in bfloat16 or wider, within the bound.
A program may use at most 64 MiB of HBM per device.

v0:
```python
import jax
import jax.numpy as jnp
from jax import lax
from jax.sharding import PartitionSpec as P

FINE = 4


def with_halo(value, sides, width):
    for axis, dim in sides:
        devices, length = (lax.axis_size(axis), value.shape[dim])
        up = [(i, (i + 1) % devices) for i in range(devices - 1)]
        down = [(j, i) for i, j in up]
        last = lax.slice_in_dim(value, length - width, length, axis=dim)
        first = lax.slice_in_dim(value, 0, width, axis=dim)
        before = lax.ppermute(last, axis, up)
        after = lax.ppermute(first, axis, down)
        value = jnp.concatenate([before, value, after], axis=dim)
    return value


def from_behind(value, axis, by):
    devices = lax.axis_size(axis)
    pairs = [(i, i + by) for i in range(devices) if 0 <= i + by < devices]
    return lax.ppermute(value, axis, pairs)


def tendency(padded, diffusivity, velocity_x, velocity_y):
    centre = padded[1:-1]
    north_row = padded[:-2]
    south_row = padded[2:]
    east_col = jnp.roll(centre, -1, axis=1)
    west_col = jnp.roll(centre, 1, axis=1)
    lapl = east_col + west_col + north_row + south_row - 4.0 * centre
    return diffusivity * lapl - 0.5 * (
        velocity_x * (east_col - west_col) + velocity_y * (south_row - north_row)
    )


def fine_step(padded, diffusivity, velocity_x, velocity_y, source):
    return padded[1:-1] + tendency(padded, diffusivity, velocity_x, velocity_y) + source


def coarse_step(padded, coef_set):
    values = padded.astype(jnp.float32)
    diff_c = coef_set[0].astype(jnp.float32)
    vel_xc = coef_set[1].astype(jnp.float32)
    vel_yc = coef_set[2].astype(jnp.float32)
    source_c = coef_set[3].astype(jnp.float32)
    return values[1:-1] + 4.0 * tendency(values, diff_c, vel_xc, vel_yc) + 4.0 * source_c


def per_device(initial, diffusivity, velocity_x, velocity_y, source):
    row_count = initial.shape[0]
    slices = lax.axis_size("tm")
    slice_index = lax.axis_index("tm")
    block_index = lax.axis_index("space")
    blocks = lax.axis_size("space")
    fine_set = (diffusivity, velocity_x, velocity_y, source)
    stacked = jnp.stack([initial.astype(jnp.bfloat16)] + [c.astype(jnp.bfloat16) for c in fine_set])
    coarse_ext = with_halo(stacked, (("space", 1),), slices)
    initial_ext = coarse_ext[0]
    coefs_ext = tuple((coarse_ext[k] for k in range(1, 5)))
    coefs_centre = tuple((c[slices : slices + row_count] for c in coefs_ext))
    global_rows = block_index * row_count - slices + jnp.arange(row_count + 2 * slices)
    inside = (global_rows >= 0) & (global_rows < blocks * row_count)
    row_mask = inside.astype(jnp.float32)[:, None]
    fine_stack = with_halo(jnp.stack(fine_set), (("space", 1),), FINE)
    fine_wide = tuple((fine_stack[k] for k in range(4)))
    fine_rows = block_index * row_count - FINE + jnp.arange(row_count + 2 * FINE)
    fine_inside = (fine_rows >= 0) & (fine_rows < blocks * row_count)
    fine_mask = fine_inside.astype(jnp.float32)[:, None]

    def fine_prop(state_field):
        wide_field = with_halo(state_field, (("space", 0),), FINE)
        for turn_idx in range(FINE):
            padded = jnp.pad(wide_field, ((1, 1), (0, 0)))
            wide_field = (
                fine_step(padded, fine_wide[0], fine_wide[1], fine_wide[2], fine_wide[3])
                * fine_mask
            )
        return wide_field[FINE : FINE + row_count]

    def own_coarse(state_ext):
        return coarse_step(state_ext[slices - 1 : slices + row_count + 1], coefs_centre)

    def advance(state_ext, delta_wide):
        padded = jnp.pad(state_ext, ((1, 1), (0, 0)))
        return ((coarse_step(padded, coefs_ext) + delta_wide) * row_mask).astype(jnp.bfloat16)

    def coarse_sweep(delta_own):
        delta_ext = with_halo(delta_own, (("space", 0),), slices)
        delta_wide = delta_ext.astype(jnp.float32)

        def relay_turn(turn_idx, begin_state):
            received = from_behind(advance(begin_state, delta_wide), "tm", 1)
            return jnp.where(slice_index == 0, initial_ext, received)

        return lax.fori_loop(0, slices - 1, relay_turn, initial_ext)

    delta_zero = (fine_prop(initial) - own_coarse(initial_ext)).astype(jnp.bfloat16)
    starts_one = coarse_sweep(delta_zero)
    start_own = starts_one[slices : slices + row_count]
    delta_one = (fine_prop(start_own.astype(jnp.float32)) - own_coarse(starts_one)).astype(
        jnp.bfloat16
    )
    starts_two = coarse_sweep(delta_one)
    end_state = own_coarse(starts_two) + delta_one.astype(jnp.float32)
    return end_state[None]


def solution(mesh):
    in_specs = (
        P(("ens", "space"), None),
        P(("ens", "space"), None),
        P(("ens", "space"), None),
        P(("ens", "space"), None),
        P(("ens", "space"), None),
    )
    out_specs = P("tm", ("ens", "space"), None)
    return jax.shard_map(
        per_device, mesh=mesh, in_specs=in_specs, out_specs=out_specs, check_vma=False
    )
```

profile of v0, /device:TPU:1, one launch (start us, length us, event | category | flops | bytes accessed | tf_op | source)
XLA Modules:
  0.0 144.1 jit_solution(12785749995403849987)
XLA Ops:
  0.0 1.9 %pad_maximum_fusion.33 = (f32[4,4,2048]{2,1,0:T(4,128)S(1)}, f32[4,4,2048]{2,1,0:T(4,128)}) fusion(f32[1,64,2048]{2,1,0:T(8,128)} %bitcast.126, f32[1,64,2048]{2,1,0:T(8,128)} %bitcast.124, f32[1,64,2048]{2,1,0:T(8,128)} %bitcast.122, f32[1,64,2048]{2,1,0:T(8,128)} %bitcast.120), kind=kLoop, calls=%fused_computation.152 | loop fusion | flops 196608 | bytes 2359296 | tf_op jit(solution)/shard_map/slice | solution.py:14
  1.9 2.1 %collective-permute-start.7 = (f32[4,4,2048]{2,1,0:T(4,128)}, f32[4,4,2048]{2,1,0:T(4,128)S(1)}, u32[]{:S(2)}, u32[]{:S(2)}) collective-permute-start(f32[4,4,2048]{2,1,0:T(4,128)} %get-tuple-element.374), channel_id=1, source_target_pairs={{1,0},{2,1},{3,2},{5,4},{6,5},{7,6},{9,8},{10,9},{11,10},{13,12},{... | collective-permute-start | bytes 393224 | tf_op jit(solution)/shard_map/ppermute | solution.py:17
  4.0 4.5 %collective-permute-start.6 = (f32[4,4,2048]{2,1,0:T(4,128)S(1)}, f32[4,4,2048]{2,1,0:T(4,128)}, u32[]{:S(2)}, u32[]{:S(2)}) collective-permute-start(f32[4,4,2048]{2,1,0:T(4,128)S(1)} %get-tuple-element.373), channel_id=1, source_target_pairs={{0,1},{1,2},{2,3},{4,5},{5,6},{6,7},{8,9},{9,10},{10,11},{12,13},{... | collective-permute-start | bytes 393224 | tf_op jit(solution)/shard_map/ppermute | solution.py:16
  8.5 1.9 %collective-permute-start.5 = (f32[4,2048]{1,0:T(4,128)S(1)}, f32[4,2048]{1,0:T(4,128)S(1)}, u32[]{:S(2)}, u32[]{:S(2)}) collective-permute-start(f32[4,2048]{1,0:T(4,128)S(1)} %get-tuple-element.433), channel_id=1, source_target_pairs={{1,0},{2,1},{3,2},{5,4},{6,5},{7,6},{9,8},{10,9},{11,10},{13,12},{... | collective-permute-start | bytes 98312 | tf_op jit(solution)/shard_map/ppermute | solution.py:17
  10.5 3.6 %collective-permute-start.4 = (f32[4,2048]{1,0:T(4,128)S(1)}, f32[4,2048]{1,0:T(4,128)S(1)}, u32[]{:S(2)}, u32[]{:S(2)}) collective-permute-start(f32[4,2048]{1,0:T(4,128)S(1)} %get-tuple-element.432), channel_id=1, source_target_pairs={{0,1},{1,2},{2,3},{4,5},{5,6},{6,7},{8,9},{9,10},{10,11},{12,13},{... | collective-permute-start | bytes 98312 | tf_op jit(solution)/shard_map/ppermute | solution.py:16
  14.1 0.7 bitcast_dynamic-update-slice_fusion.4
  14.8 0.8 bitcast_dynamic-update-slice_fusion.3
  15.6 0.8 bitcast_dynamic-update-slice_fusion.2
  16.4 0.9 bitcast_dynamic-update-slice_fusion.1
  17.3 0.9 bitcast_dynamic-update-slice_fusion
  18.1 1.1 fusion.43
  19.3 1.9 %collective-permute-start.3 = (bf16[5,4,2048]{2,1,0:T(4,128)(2,1)S(1)}, bf16[5,4,2048]{2,1,0:T(4,128)(2,1)S(1)}, u32[]{:S(2)}, u32[]{:S(2)}) collective-permute-start(bf16[5,4,2048]{2,1,0:T(4,128)(2,1)S(1)} %get-tuple-element.385), channel_id=1, source_target_pairs={{1,0},{2,1},{3,2},{5,4},{6,5},{7,6},{9,8},{10,9},{11,10},{13,12},{... | collective-permute-start | bytes 245768 | tf_op jit(solution)/shard_map/ppermute | solution.py:17
  21.2 3.6 %collective-permute-start.2 = (bf16[5,4,2048]{2,1,0:T(4,128)(2,1)S(1)}, bf16[5,4,2048]{2,1,0:T(4,128)(2,1)S(1)}, u32[]{:S(2)}, u32[]{:S(2)}) collective-permute-start(bf16[5,4,2048]{2,1,0:T(4,128)(2,1)S(1)} %get-tuple-element.384), channel_id=1, source_target_pairs={{0,1},{1,2},{2,3},{4,5},{5,6},{6,7},{8,9},{9,10},{10,11},{12,13},{... | collective-permute-start | bytes 245768 | tf_op jit(solution)/shard_map/ppermute | solution.py:16
  25.3 1.1 collective-permute-done.2
  26.3 1.7 %pad_maximum_fusion.5 = bf16[5,72,2048]{2,1,0:T(8,128)(2,1)S(1)} fusion(bf16[5,4,2048]{2,1,0:T(4,128)(2,1)S(1)} %collective-permute-done.3, bf16[5,64,2048]{2,1,0:T(8,128)(2,1)} %get-tuple-element.351, bf16[5,4,2048]{2,1,0:T(4,128)(2,1)S(1)} %collective-permute-done.2), kind=kLoop, calls=%fused_computation.21 | loop fusion | flops 4423680 | bytes 2949120 | tf_op jit(solution)/shard_map/concatenate | solution.py:18
  28.6 0.6 copy-done.32
  29.5 1.3 pad_maximum_fusion.4
  31.6 0.5 add_multiply_fusion.4
  32.4 0.5 broadcast_multiply_fusion.1
  34.8 1.0 fusion.11
  35.8 1.9 %collective-permute-start.9 = (bf16[4,2048]{1,0:T(4,128)(2,1)S(1)}, bf16[4,2048]{1,0:T(4,128)(2,1)S(1)}, u32[]{:S(2)}, u32[]{:S(2)}) collective-permute-start(bf16[4,2048]{1,0:T(4,128)(2,1)S(1)} %get-tuple-element.437), channel_id=1, source_target_pairs={{1,0},{2,1},{3,2},{5,4},{6,5},{7,6},{9,8},{10,9},{11,10},{13,12},{... | collective-permute-start | bytes 49160 | tf_op jit(solution)/shard_map/ppermute | solution.py:17
  37.7 4.3 %collective-permute-start.8 = (bf16[4,2048]{1,0:T(4,128)(2,1)S(1)}, bf16[4,2048]{1,0:T(4,128)(2,1)S(1)}, u32[]{:S(2)}, u32[]{:S(2)}) collective-permute-start(bf16[4,2048]{1,0:T(4,128)(2,1)S(1)} %get-tuple-element.436), channel_id=1, source_target_pairs={{0,1},{1,2},{2,3},{4,5},{5,6},{6,7},{8,9},{9,10},{10,11},{12,13},{... | collective-permute-start | bytes 49160 | tf_op jit(solution)/shard_map/ppermute | solution.py:16
  42.0 0.9 slice_bitcast_fusion.7
  43.0 0.9 maximum_convert_fusion
  43.9 41.6 %while.26 = (s32[]{:T(128)}, bf16[72,2048]{1,0:T(8,128)(2,1)S(1)}, pred[]{:T(512)}, bf16[72,2048]{1,0:T(8,128)(2,1)}, bf16[72,2048]{1,0:T(8,128)(2,1)}, /*index=...) while((s32[]{:T(128)}, bf16[72,2048]{1,0:T(8,128)(2,1)S(1)}, ...), condition=%wide.region_1.2_spmd.clone, body=%wide.region_0.1_spmd.clone.sunk | while | flops 4133370 | bytes 16531722 | solution.py:99
  44.3 0.6 copy-done
  45.1 1.4 multiply_convert_fusion.4
  46.5 3.2 %collective-permute-start = (bf16[72,2048]{1,0:T(8,128)(2,1)}, bf16[72,2048]{1,0:T(8,128)(2,1)S(1)}, u32[]{:S(2)}, u32[]{:S(2)}) collective-permute-start(bf16[72,2048]{1,0:T(8,128)(2,1)} %multiply_convert_fusion.4), channel_id=1, source_target_pairs={{0,4},{4,8},{8,12},{1,5},{5,9},{9,13},{2,6},{6,10},{10,14},{3,7},{... | collective-permute-start | bytes 884744 | tf_op jit(solution)/shard_map/while/body/eval_jaxpr/ppermute | solution.py:25
  49.7 5.7 %collective-permute-done = bf16[72,2048]{1,0:T(8,128)(2,1)S(1)} collective-permute-done((bf16[72,2048]{1,0:T(8,128)(2,1)}, bf16[72,2048]{1,0:T(8,128)(2,1)S(1)}, u32[]{:S(2)}, u32[]{:S(2)}) %collective-permute-start) | collective-permute-done | bytes 294944 | tf_op jit(solution)/shard_map/while/body/eval_jaxpr/ppermute | solution.py:25
  55.4 0.7 copy-done.6
  56.6 0.5 copy-done
  57.5 1.4 multiply_convert_fusion.4
  58.9 4.7 %collective-permute-start = (bf16[72,2048]{1,0:T(8,128)(2,1)}, bf16[72,2048]{1,0:T(8,128)(2,1)S(1)}, u32[]{:S(2)}, u32[]{:S(2)}) collective-permute-start(bf16[72,2048]{1,0:T(8,128)(2,1)} %multiply_convert_fusion.4), channel_id=1, source_target_pairs={{0,4},{4,8},{8,12},{1,5},{5,9},{9,13},{2,6},{6,10},{10,14},{3,7},{... | collective-permute-start | bytes 884744 | tf_op jit(solution)/shard_map/while/body/eval_jaxpr/ppermute | solution.py:25
  63.5 6.8 %collective-permute-done = bf16[72,2048]{1,0:T(8,128)(2,1)S(1)} collective-permute-done((bf16[72,2048]{1,0:T(8,128)(2,1)}, bf16[72,2048]{1,0:T(8,128)(2,1)S(1)}, u32[]{:S(2)}, u32[]{:S(2)}) %collective-permute-start) | collective-permute-done | bytes 294944 | tf_op jit(solution)/shard_map/while/body/eval_jaxpr/ppermute | solution.py:25
  70.3 0.7 copy-done.6
  72.3 1.4 multiply_convert_fusion.4
  73.7 4.7 %collective-permute-start = (bf16[72,2048]{1,0:T(8,128)(2,1)}, bf16[72,2048]{1,0:T(8,128)(2,1)S(1)}, u32[]{:S(2)}, u32[]{:S(2)}) collective-permute-start(bf16[72,2048]{1,0:T(8,128)(2,1)} %multiply_convert_fusion.4), channel_id=1, source_target_pairs={{0,4},{4,8},{8,12},{1,5},{5,9},{9,13},{2,6},{6,10},{10,14},{3,7},{... | collective-permute-start | bytes 884744 | tf_op jit(solution)/shard_map/while/body/eval_jaxpr/ppermute | solution.py:25
  78.4 6.3 %collective-permute-done = bf16[72,2048]{1,0:T(8,128)(2,1)S(1)} collective-permute-done((bf16[72,2048]{1,0:T(8,128)(2,1)}, bf16[72,2048]{1,0:T(8,128)(2,1)S(1)}, u32[]{:S(2)}, u32[]{:S(2)}) %collective-permute-start) | collective-permute-done | bytes 294944 | tf_op jit(solution)/shard_map/while/body/eval_jaxpr/ppermute | solution.py:25
  84.7 0.7 copy-done.6
  85.7 3.1 %collective-permute-start.11 = (f32[4,2048]{1,0:T(4,128)S(1)}, f32[4,2048]{1,0:T(4,128)S(1)}, u32[]{:S(2)}, u32[]{:S(2)}) collective-permute-start(f32[4,2048]{1,0:T(4,128)S(1)} %get-tuple-element.431), channel_id=1, source_target_pairs={{1,0},{2,1},{3,2},{5,4},{6,5},{7,6},{9,8},{10,9},{11,10},{13,12},{... | collective-permute-start | bytes 98312 | tf_op jit(solution)/shard_map/ppermute | solution.py:17
  88.8 2.6 %collective-permute-start.10 = (f32[4,2048]{1,0:T(4,128)S(1)}, f32[4,2048]{1,0:T(4,128)S(1)}, u32[]{:S(2)}, u32[]{:S(2)}) collective-permute-start(f32[4,2048]{1,0:T(4,128)S(1)} %get-tuple-element.430), channel_id=1, source_target_pairs={{0,1},{1,2},{2,3},{4,5},{5,6},{6,7},{8,9},{9,10},{10,11},{12,13},{... | collective-permute-start | bytes 98312 | tf_op jit(solution)/shard_map/ppermute | solution.py:16
  92.6 0.5 add_multiply_fusion.2
  94.3 0.5 broadcast_multiply_fusion
  95.6 0.6 copy-done.15
  96.7 1.0 fusion.17
  97.7 1.9 %collective-permute-start.13 = (bf16[4,2048]{1,0:T(4,128)(2,1)S(1)}, bf16[4,2048]{1,0:T(4,128)(2,1)S(1)}, u32[]{:S(2)}, u32[]{:S(2)}) collective-permute-start(bf16[4,2048]{1,0:T(4,128)(2,1)S(1)} %get-tuple-element.435), channel_id=1, source_target_pairs={{1,0},{2,1},{3,2},{5,4},{6,5},{7,6},{9,8},{10,9},{11,10},{13,12},{... | collective-permute-start | bytes 49160 | tf_op jit(solution)/shard_map/ppermute | solution.py:17
  99.6 4.2 %collective-permute-start.12 = (bf16[4,2048]{1,0:T(4,128)(2,1)S(1)}, bf16[4,2048]{1,0:T(4,128)(2,1)S(1)}, u32[]{:S(2)}, u32[]{:S(2)}) collective-permute-start(bf16[4,2048]{1,0:T(4,128)(2,1)S(1)} %get-tuple-element.434), channel_id=1, source_target_pairs={{0,1},{1,2},{2,3},{4,5},{5,6},{6,7},{8,9},{9,10},{10,11},{12,13},{... | collective-permute-start | bytes 49160 | tf_op jit(solution)/shard_map/ppermute | solution.py:16
  103.9 0.8 collective-permute-done.12
  104.7 0.9 maximum_convert_fusion.1
  105.6 35.9 %while.27 = (s32[]{:T(128)}, bf16[72,2048]{1,0:T(8,128)(2,1)S(1)}, pred[]{:T(512)}, bf16[72,2048]{1,0:T(8,128)(2,1)S(1)}, bf16[72,2048]{1,0:T(8,128)(2,1)S(1)}, ...) while((s32[]{:T(128)}, bf16[72,2048]{1,0:T(8,128)(2,1)S(1)}, ...), condition=%wide.region_3.4_spmd.clone, body=%wide.region_2.3_spmd.clone.sunk | while | flops 4133370 | bytes 12992694 | solution.py:99
  106.0 0.7 copy-done.4
  106.7 0.7 multiply_convert_fusion.5
  107.3 5.0 %collective-permute-start.1 = (bf16[72,2048]{1,0:T(8,128)(2,1)S(1)}, bf16[72,2048]{1,0:T(8,128)(2,1)S(1)}, u32[]{:S(2)}, u32[]{:S(2)}) collective-permute-start(bf16[72,2048]{1,0:T(8,128)(2,1)S(1)} %multiply_convert_fusion.5), channel_id=1, source_target_pairs={{0,4},{4,8},{8,12},{1,5},{5,9},{9,13},{2,6},{6,10},{10,14},{3,7},{... | collective-permute-start | bytes 884744 | tf_op jit(solution)/shard_map/while/body/eval_jaxpr/ppermute | solution.py:25
  112.3 5.4 %collective-permute-done.1 = bf16[72,2048]{1,0:T(8,128)(2,1)S(1)} collective-permute-done((bf16[72,2048]{1,0:T(8,128)(2,1)S(1)}, bf16[72,2048]{1,0:T(8,128)(2,1)S(1)}, u32[]{:S(2)}, u32[]{:S(2)}) %collective-permute-start.1) | collective-permute-done | bytes 294944 | tf_op jit(solution)/shard_map/while/body/eval_jaxpr/ppermute | solution.py:25
  118.2 0.7 copy-done.4
  118.9 0.7 multiply_convert_fusion.5
  119.5 3.8 %collective-permute-start.1 = (bf16[72,2048]{1,0:T(8,128)(2,1)S(1)}, bf16[72,2048]{1,0:T(8,128)(2,1)S(1)}, u32[]{:S(2)}, u32[]{:S(2)}) collective-permute-start(bf16[72,2048]{1,0:T(8,128)(2,1)S(1)} %multiply_convert_fusion.5), channel_id=1, source_target_pairs={{0,4},{4,8},{8,12},{1,5},{5,9},{9,13},{2,6},{6,10},{10,14},{3,7},{... | collective-permute-start | bytes 884744 | tf_op jit(solution)/shard_map/while/body/eval_jaxpr/ppermute | solution.py:25
  123.4 6.5 %collective-permute-done.1 = bf16[72,2048]{1,0:T(8,128)(2,1)S(1)} collective-permute-done((bf16[72,2048]{1,0:T(8,128)(2,1)S(1)}, bf16[72,2048]{1,0:T(8,128)(2,1)S(1)}, u32[]{:S(2)}, u32[]{:S(2)}) %collective-permute-start.1) | collective-permute-done | bytes 294944 | tf_op jit(solution)/shard_map/while/body/eval_jaxpr/ppermute | solution.py:25
  130.4 0.7 copy-done.4
  131.0 0.7 multiply_convert_fusion.5
  131.7 3.8 %collective-permute-start.1 = (bf16[72,2048]{1,0:T(8,128)(2,1)S(1)}, bf16[72,2048]{1,0:T(8,128)(2,1)S(1)}, u32[]{:S(2)}, u32[]{:S(2)}) collective-permute-start(bf16[72,2048]{1,0:T(8,128)(2,1)S(1)} %multiply_convert_fusion.5), channel_id=1, source_target_pairs={{0,4},{4,8},{8,12},{1,5},{5,9},{9,13},{2,6},{6,10},{10,14},{3,7},{... | collective-permute-start | bytes 884744 | tf_op jit(solution)/shard_map/while/body/eval_jaxpr/ppermute | solution.py:25
  135.5 6.0 %collective-permute-done.1 = bf16[72,2048]{1,0:T(8,128)(2,1)S(1)} collective-permute-done((bf16[72,2048]{1,0:T(8,128)(2,1)S(1)}, bf16[72,2048]{1,0:T(8,128)(2,1)S(1)}, u32[]{:S(2)}, u32[]{:S(2)}) %collective-permute-start.1) | collective-permute-done | bytes 294944 | tf_op jit(solution)/shard_map/while/body/eval_jaxpr/ppermute | solution.py:25
  141.9 0.5 copy-done.22
  142.7 1.3 fusion.23
  (156 shorter events, 12.3 us)
Async XLA Ops:
  0.0 15.6 %copy-start.8 = (f32[64,2048]{1,0:T(8,128)S(1)}, f32[64,2048]{1,0:T(8,128)}, u32[]{:S(2)}) copy-start(f32[64,2048]{1,0:T(8,128)} %param.11) | copy-start | bytes 1572868
  0.0 14.8 %copy-start.7 = (f32[64,2048]{1,0:T(8,128)S(1)}, f32[64,2048]{1,0:T(8,128)}, u32[]{:S(2)}) copy-start(f32[64,2048]{1,0:T(8,128)} %param.10) | copy-start | bytes 1572868
  0.0 8.5 %copy-start.31 = (f32[64,2048]{1,0:T(8,128)S(1)}, f32[64,2048]{1,0:T(8,128)}, u32[]{:S(2)}) copy-start(f32[64,2048]{1,0:T(8,128)} %param.9) | copy-start | bytes 1572868
  0.0 16.4 %copy-start.10 = (f32[64,2048]{1,0:T(8,128)S(1)}, f32[64,2048]{1,0:T(8,128)}, u32[]{:S(2)}) copy-start(f32[64,2048]{1,0:T(8,128)} %param.12) | copy-start | bytes 1572868
  1.9 15.3 %copy-start.12 = (f32[64,2048]{1,0:T(8,128)S(1)}, f32[64,2048]{1,0:T(8,128)}, u32[]{:S(2)}) copy-start(f32[64,2048]{1,0:T(8,128)} %param.13) | copy-start | bytes 1572868
  1.9 26.6 %collective-permute-start.7 = (f32[4,4,2048]{2,1,0:T(4,128)}, f32[4,4,2048]{2,1,0:T(4,128)S(1)}, u32[]{:S(2)}, u32[]{:S(2)}) collective-permute-start(f32[4,4,2048]{2,1,0:T(4,128)} %get-tuple-element.374), channel_id=1, source_target_pairs={{1,0},{2,1},{3,2},{5,4},{6,5},{7,6},{9,8},{10,9},{11,10},{13,12},{... | collective-permute-start | bytes 393224 | tf_op jit(solution)/shard_map/ppermute | solution.py:17
  4.0 25.2 %collective-permute-start.6 = (f32[4,4,2048]{2,1,0:T(4,128)S(1)}, f32[4,4,2048]{2,1,0:T(4,128)}, u32[]{:S(2)}, u32[]{:S(2)}) collective-permute-start(f32[4,4,2048]{2,1,0:T(4,128)S(1)} %get-tuple-element.373), channel_id=1, source_target_pairs={{0,1},{1,2},{2,3},{4,5},{5,6},{6,7},{8,9},{9,10},{10,11},{12,13},{... | collective-permute-start | bytes 393224 | tf_op jit(solution)/shard_map/ppermute | solution.py:16
  8.5 12.7 %collective-permute-start.5 = (f32[4,2048]{1,0:T(4,128)S(1)}, f32[4,2048]{1,0:T(4,128)S(1)}, u32[]{:S(2)}, u32[]{:S(2)}) collective-permute-start(f32[4,2048]{1,0:T(4,128)S(1)} %get-tuple-element.433), channel_id=1, source_target_pairs={{1,0},{2,1},{3,2},{5,4},{6,5},{7,6},{9,8},{10,9},{11,10},{13,12},{... | collective-permute-start | bytes 98312 | tf_op jit(solution)/shard_map/ppermute | solution.py:17
  10.5 14.4 %collective-permute-start.4 = (f32[4,2048]{1,0:T(4,128)S(1)}, f32[4,2048]{1,0:T(4,128)S(1)}, u32[]{:S(2)}, u32[]{:S(2)}) collective-permute-start(f32[4,2048]{1,0:T(4,128)S(1)} %get-tuple-element.432), channel_id=1, source_target_pairs={{0,1},{1,2},{2,3},{4,5},{5,6},{6,7},{8,9},{9,10},{10,11},{12,13},{... | collective-permute-start | bytes 98312 | tf_op jit(solution)/shard_map/ppermute | solution.py:16
  15.6 18.3 %copy-start.18 = (bf16[64,2048]{1,0:T(8,128)(2,1)}, bf16[64,2048]{1,0:T(8,128)(2,1)S(1)}, u32[]{:S(2)}) copy-start(bf16[64,2048]{1,0:T(8,128)(2,1)S(1)} %get-tuple-element.358) | copy-start | bytes 786436
  16.4 17.5 %copy-start.20 = (bf16[64,2048]{1,0:T(8,128)(2,1)}, bf16[64,2048]{1,0:T(8,128)(2,1)S(1)}, u32[]{:S(2)}) copy-start(bf16[64,2048]{1,0:T(8,128)(2,1)S(1)} %get-tuple-element.356) | copy-start | bytes 786436
  19.3 6.0 %collective-permute-start.3 = (bf16[5,4,2048]{2,1,0:T(4,128)(2,1)S(1)}, bf16[5,4,2048]{2,1,0:T(4,128)(2,1)S(1)}, u32[]{:S(2)}, u32[]{:S(2)}) collective-permute-start(bf16[5,4,2048]{2,1,0:T(4,128)(2,1)S(1)} %get-tuple-element.385), channel_id=1, source_target_pairs={{1,0},{2,1},{3,2},{5,4},{6,5},{7,6},{9,8},{10,9},{11,10},{13,12},{... | collective-permute-start | bytes 245768 | tf_op jit(solution)/shard_map/ppermute | solution.py:17
  21.2 5.1 %collective-permute-start.2 = (bf16[5,4,2048]{2,1,0:T(4,128)(2,1)S(1)}, bf16[5,4,2048]{2,1,0:T(4,128)(2,1)S(1)}, u32[]{:S(2)}, u32[]{:S(2)}) collective-permute-start(bf16[5,4,2048]{2,1,0:T(4,128)(2,1)S(1)} %get-tuple-element.384), channel_id=1, source_target_pairs={{0,1},{1,2},{2,3},{4,5},{5,6},{6,7},{8,9},{9,10},{10,11},{12,13},{... | collective-permute-start | bytes 245768 | tf_op jit(solution)/shard_map/ppermute | solution.py:16
  28.1 1.1 copy-start.9
  28.1 1.2 copy-start.11
  28.1 1.3 copy-start.13
  28.6 0.7 copy-start.32
  33.4 0.8 copy-start.14
  33.4 1.0 copy-start.16
  33.4 1.2 copy-start.23
  33.4 1.4 copy-start.26
  35.8 7.2 %collective-permute-start.9 = (bf16[4,2048]{1,0:T(4,128)(2,1)S(1)}, bf16[4,2048]{1,0:T(4,128)(2,1)S(1)}, u32[]{:S(2)}, u32[]{:S(2)}) collective-permute-start(bf16[4,2048]{1,0:T(4,128)(2,1)S(1)} %get-tuple-element.437), channel_id=1, source_target_pairs={{1,0},{2,1},{3,2},{5,4},{6,5},{7,6},{9,8},{10,9},{11,10},{13,12},{... | collective-permute-start | bytes 49160 | tf_op jit(solution)/shard_map/ppermute | solution.py:17
  37.7 5.2 %collective-permute-start.8 = (bf16[4,2048]{1,0:T(4,128)(2,1)S(1)}, bf16[4,2048]{1,0:T(4,128)(2,1)S(1)}, u32[]{:S(2)}, u32[]{:S(2)}) collective-permute-start(bf16[4,2048]{1,0:T(4,128)(2,1)S(1)} %get-tuple-element.436), channel_id=1, source_target_pairs={{0,1},{1,2},{2,3},{4,5},{5,6},{6,7},{8,9},{9,10},{10,11},{12,13},{... | collective-permute-start | bytes 49160 | tf_op jit(solution)/shard_map/ppermute | solution.py:16
  43.9 1.0 copy-start
  43.9 1.0 copy-start.2
  43.9 1.2 copy-start.5
  46.5 8.9 %collective-permute-start = (bf16[72,2048]{1,0:T(8,128)(2,1)}, bf16[72,2048]{1,0:T(8,128)(2,1)S(1)}, u32[]{:S(2)}, u32[]{:S(2)}) collective-permute-start(bf16[72,2048]{1,0:T(8,128)(2,1)} %multiply_convert_fusion.4), channel_id=1, source_target_pairs={{0,4},{4,8},{8,12},{1,5},{5,9},{9,13},{2,6},{6,10},{10,14},{3,7},{... | collective-permute-start | bytes 884744 | tf_op jit(solution)/shard_map/while/body/eval_jaxpr/ppermute | solution.py:25
  55.4 0.7 copy-start.6
  56.2 1.0 copy-start
  56.2 1.0 copy-start.2
  56.2 1.2 copy-start.5
  58.9 11.5 %collective-permute-start = (bf16[72,2048]{1,0:T(8,128)(2,1)}, bf16[72,2048]{1,0:T(8,128)(2,1)S(1)}, u32[]{:S(2)}, u32[]{:S(2)}) collective-permute-start(bf16[72,2048]{1,0:T(8,128)(2,1)} %multiply_convert_fusion.4), channel_id=1, source_target_pairs={{0,4},{4,8},{8,12},{1,5},{5,9},{9,13},{2,6},{6,10},{10,14},{3,7},{... | collective-permute-start | bytes 884744 | tf_op jit(solution)/shard_map/while/body/eval_jaxpr/ppermute | solution.py:25
  70.3 0.7 copy-start.6
  71.1 1.0 copy-start
  71.1 1.0 copy-start.2
  71.1 1.2 copy-start.5
  73.7 11.0 %collective-permute-start = (bf16[72,2048]{1,0:T(8,128)(2,1)}, bf16[72,2048]{1,0:T(8,128)(2,1)S(1)}, u32[]{:S(2)}, u32[]{:S(2)}) collective-permute-start(bf16[72,2048]{1,0:T(8,128)(2,1)} %multiply_convert_fusion.4), channel_id=1, source_target_pairs={{0,4},{4,8},{8,12},{1,5},{5,9},{9,13},{2,6},{6,10},{10,14},{3,7},{... | collective-permute-start | bytes 884744 | tf_op jit(solution)/shard_map/while/body/eval_jaxpr/ppermute | solution.py:25
  84.7 0.7 copy-start.6
  85.7 6.1 %collective-permute-start.11 = (f32[4,2048]{1,0:T(4,128)S(1)}, f32[4,2048]{1,0:T(4,128)S(1)}, u32[]{:S(2)}, u32[]{:S(2)}) collective-permute-start(f32[4,2048]{1,0:T(4,128)S(1)} %get-tuple-element.431), channel_id=1, source_target_pairs={{1,0},{2,1},{3,2},{5,4},{6,5},{7,6},{9,8},{10,9},{11,10},{13,12},{... | collective-permute-start | bytes 98312 | tf_op jit(solution)/shard_map/ppermute | solution.py:17
  88.8 3.5 %collective-permute-start.10 = (f32[4,2048]{1,0:T(4,128)S(1)}, f32[4,2048]{1,0:T(4,128)S(1)}, u32[]{:S(2)}, u32[]{:S(2)}) collective-permute-start(f32[4,2048]{1,0:T(4,128)S(1)} %get-tuple-element.430), channel_id=1, source_target_pairs={{0,1},{1,2},{2,3},{4,5},{5,6},{6,7},{8,9},{9,10},{10,11},{12,13},{... | collective-permute-start | bytes 98312 | tf_op jit(solution)/shard_map/ppermute | solution.py:16
  95.1 1.1 copy-start.15
  95.1 1.2 copy-start.17
  95.1 1.3 copy-start.19
  95.1 1.4 copy-start.21
  95.1 1.4 %copy-start.24 = (bf16[64,2048]{1,0:T(8,128)(2,1)S(1)}, bf16[64,2048]{1,0:T(8,128)(2,1)}, u32[]{:S(2)}) copy-start(bf16[64,2048]{1,0:T(8,128)(2,1)} %get-tuple-element.354) | copy-start | bytes 786436
  95.2 1.5 %copy-start.27 = (bf16[64,2048]{1,0:T(8,128)(2,1)S(1)}, bf16[64,2048]{1,0:T(8,128)(2,1)}, u32[]{:S(2)}) copy-start(bf16[64,2048]{1,0:T(8,128)(2,1)} %get-tuple-element.352) | copy-start | bytes 786436
  96.7 8.9 %copy-start.1 = (bf16[72,2048]{1,0:T(8,128)(2,1)S(1)}, bf16[72,2048]{1,0:T(8,128)(2,1)}, u32[]{:S(2)}) copy-start(bf16[72,2048]{1,0:T(8,128)(2,1)} %get-tuple-element.645) | copy-start | bytes 884740
  96.7 8.9 %copy-start.3 = (bf16[72,2048]{1,0:T(8,128)(2,1)S(1)}, bf16[72,2048]{1,0:T(8,128)(2,1)}, u32[]{:S(2)}) copy-start(bf16[72,2048]{1,0:T(8,128)(2,1)} %get-tuple-element.646) | copy-start | bytes 884740
  97.6 8.0 %copy-start.29 = (bf16[64,2048]{1,0:T(8,128)(2,1)}, bf16[64,2048]{1,0:T(8,128)(2,1)S(1)}, u32[]{:S(2)}) copy-start(bf16[64,2048]{1,0:T(8,128)(2,1)S(1)} %fusion.17) | copy-start | bytes 786436
  97.7 6.2 %collective-permute-start.13 = (bf16[4,2048]{1,0:T(4,128)(2,1)S(1)}, bf16[4,2048]{1,0:T(4,128)(2,1)S(1)}, u32[]{:S(2)}, u32[]{:S(2)}) collective-permute-start(bf16[4,2048]{1,0:T(4,128)(2,1)S(1)} %get-tuple-element.435), channel_id=1, source_target_pairs={{1,0},{2,1},{3,2},{5,4},{6,5},{7,6},{9,8},{10,9},{11,10},{13,12},{... | collective-permute-start | bytes 49160 | tf_op jit(solution)/shard_map/ppermute | solution.py:17
  99.6 5.1 %collective-permute-start.12 = (bf16[4,2048]{1,0:T(4,128)(2,1)S(1)}, bf16[4,2048]{1,0:T(4,128)(2,1)S(1)}, u32[]{:S(2)}, u32[]{:S(2)}) collective-permute-start(bf16[4,2048]{1,0:T(4,128)(2,1)S(1)} %get-tuple-element.434), channel_id=1, source_target_pairs={{0,1},{1,2},{2,3},{4,5},{5,6},{6,7},{8,9},{9,10},{10,11},{12,13},{... | collective-permute-start | bytes 49160 | tf_op jit(solution)/shard_map/ppermute | solution.py:16
  105.6 1.1 copy-start.4
  107.3 10.4 %collective-permute-start.1 = (bf16[72,2048]{1,0:T(8,128)(2,1)S(1)}, bf16[72,2048]{1,0:T(8,128)(2,1)S(1)}, u32[]{:S(2)}, u32[]{:S(2)}) collective-permute-start(bf16[72,2048]{1,0:T(8,128)(2,1)S(1)} %multiply_convert_fusion.5), channel_id=1, source_target_pairs={{0,4},{4,8},{8,12},{1,5},{5,9},{9,13},{2,6},{6,10},{10,14},{3,7},{... | collective-permute-start | bytes 884744 | tf_op jit(solution)/shard_map/while/body/eval_jaxpr/ppermute | solution.py:25
  117.8 1.1 copy-start.4
  119.5 10.4 %collective-permute-start.1 = (bf16[72,2048]{1,0:T(8,128)(2,1)S(1)}, bf16[72,2048]{1,0:T(8,128)(2,1)S(1)}, u32[]{:S(2)}, u32[]{:S(2)}) collective-permute-start(bf16[72,2048]{1,0:T(8,128)(2,1)S(1)} %multiply_convert_fusion.5), channel_id=1, source_target_pairs={{0,4},{4,8},{8,12},{1,5},{5,9},{9,13},{2,6},{6,10},{10,14},{3,7},{... | collective-permute-start | bytes 884744 | tf_op jit(solution)/shard_map/while/body/eval_jaxpr/ppermute | solution.py:25
  129.9 1.1 copy-start.4
  131.7 9.8 %collective-permute-start.1 = (bf16[72,2048]{1,0:T(8,128)(2,1)S(1)}, bf16[72,2048]{1,0:T(8,128)(2,1)S(1)}, u32[]{:S(2)}, u32[]{:S(2)}) collective-permute-start(bf16[72,2048]{1,0:T(8,128)(2,1)S(1)} %multiply_convert_fusion.5), channel_id=1, source_target_pairs={{0,4},{4,8},{8,12},{1,5},{5,9},{9,13},{2,6},{6,10},{10,14},{3,7},{... | collective-permute-start | bytes 884744 | tf_op jit(solution)/shard_map/while/body/eval_jaxpr/ppermute | solution.py:25
  141.5 1.0 copy-start.22
  141.5 1.0 copy-start.25
  141.6 1.1 copy-start.28
  141.6 1.2 copy-start.30
where the time goes:
time: 146 us; the launch traced here: 144 us
  starting transfers between devices  61 us (42%)
  waiting for transfers between devices  39.1 us (27%)
  other arithmetic  25.9 us (18%)
  local copies, waits for them, and re-layouts  17.2 us (12%)
    ppermute x6, waiting for transfers between devices, from_behind(): return lax.ppermute(value, axis, pairs)  36.7 us
    ppermute x6, starting transfers between devices, from_behind(): return lax.ppermute(value, axis, pairs)  25.2 us
    ppermute x6, starting transfers between devices, with_halo(): before = lax.ppermute(last, axis, up)  22.9 us
    ppermute x6, starting transfers between devices, with_halo(): after = lax.ppermute(first, axis, down)  12.8 us
    while x30, local copies, waits for them, and re-layouts  6.63 us
    convert_element_type x6, other arithmetic, advance(): ((coarse_step(padded, coefs_ext) + delta_wide) * row_mask).astype(jnp.bfl...  6.18 us
    slice x28, local copies, waits for them, and re-layouts, tendency(): east_col = jnp.roll(centre, -1, axis=1)  4.62 us
    unnamed x58, local copies, waits for them, and re-layouts  3.78 us
  transfers between devices with their start and end apart: 18, of which 9 were waited for; matrix products, arithmetic and copies ran while one was open for 6% of the time, Pallas kernels for 0%

commit v1 on v0

v1 whole, which is shorter than its diff:
```python
import functools
from fractions import Fraction

import jax
import jax.numpy as jnp
from jax import lax
from jax.experimental import pallas as pl
from jax.experimental.pallas import tpu as pltpu
from jax.sharding import PartitionSpec as P

FINE = 4
TILE = 8
MESH = pl.DeviceIdType.MESH


def poly_add(a, b, sign=1):
    size = max(len(a), len(b))
    a, b = (list(x) + [Fraction(0)] * (size - len(x)) for x in (a, b))
    return [x + sign * y for x, y in zip(a, b)]


def poly_mul(a, b):
    out = [Fraction(0)] * (len(a) + len(b) - 1)
    for i, x in enumerate(a):
        for j, y in enumerate(b):
            out[i + j] += x * y
    return out


def end_polynomials(slices):
    fine_step = [Fraction(FINE - 1, FINE), Fraction(1, FINE)]
    power, total = [Fraction(1)], [Fraction(0)]
    for _ in range(FINE):
        total = poly_add(total, power)
        power = poly_mul(power, fine_step)

    def fine(q):
        return poly_add(poly_mul(power, q), total)

    def coarse(q):
        return poly_add([Fraction(0)] + list(q), [Fraction(FINE)])

    start_one = start_two = [Fraction(0)]
    delta_zero = poly_add(fine(start_one), coarse(start_one), -1)
    ends = []
    for _ in range(slices):
        delta_one = poly_add(fine(start_one), coarse(start_one), -1)
        start_two = poly_add(coarse(start_two), delta_one)
        ends.append(list(start_two))
        start_one = poly_add(coarse(start_one), delta_zero)
    for q in ends:
        while len(q) > 1 and q[-1] == 0:
            q.pop()
    degree = max(len(q) for q in ends) - 1
    return [[float(c) for c in q] + [0.0] * (degree + 1 - len(q)) for q in ends]


def neighbours(centre, above, below):
    rows, cols = centre.shape
    sub = lax.broadcasted_iota(jnp.int32, (rows, cols), 0)
    east = pltpu.roll(centre, cols - 1, 1)
    west = pltpu.roll(centre, 1, 1)
    north = pltpu.roll(jnp.where(sub == rows - 1, above, centre), 1, 0)
    south = pltpu.roll(jnp.where(sub == 0, below, centre), rows - 1, 0)
    return east, west, north, south


def kernel(table, halo, pad, blocks, *refs):
    args, out_ref = refs[:5], refs[5]
    raw, wts, g_ref, y_ref, send, recv, in_sem, send_sem, recv_sem = refs[6:]
    rows, cols = args[0].shape
    tiles = (rows + 2 * pad) // TILE
    first, last = pad // TILE, (pad + rows) // TILE
    degree = len(table[0]) - 1
    me, turn = lax.axis_index("space"), lax.axis_index("tm")
    has = (me > 0, me < blocks - 1)
    peer = (me - 1, me + 1)

    loads = [
        pltpu.make_async_copy(args[a], raw.at[a, pl.ds(pad, rows)], in_sem.at[a])
        for a in range(5)
    ]
    for load in loads:
        load.start()
    barrier = pltpu.get_barrier_semaphore()
    for side in range(2):
        @pl.when(has[side])
        def _():
            pl.semaphore_signal(
                barrier, inc=1, device_id={"space": peer[side]}, device_id_type=MESH
            )

    def remote(side, slot):
        return pltpu.make_async_remote_copy(
            src_ref=send.at[side],
            dst_ref=recv.at[slot],
            send_sem=send_sem.at[side],
            recv_sem=recv_sem.at[slot],
            device_id={"space": peer[side]},
            device_id_type=MESH,
        )

    for a in range(5):
        loads[a].wait()
        send[0, a] = raw[a, pl.ds(pad, pad), :].astype(jnp.bfloat16)
        send[1, a] = raw[a, pl.ds(rows, pad), :].astype(jnp.bfloat16)
    peers = has[0].astype(jnp.int32) + has[1].astype(jnp.int32)
    pl.semaphore_wait(barrier, peers)
    for side in range(2):
        @pl.when(has[side])
        def _():
            remote(side, 1 - side).start()

    def at(t):
        return pl.ds(pl.multiple_of(t * TILE, TILE), TILE)

    def trio(ref, t):
        return (
            ref[at(t), :],
            ref[at(jnp.maximum(t - 1, 0)), :],
            ref[at(jnp.minimum(t + 1, tiles - 1)), :],
        )

    def apply(centre, around, w):
        east, west, north, south = around
        return (w[0] * east + w[1] * west) + (w[2] * north + w[3] * south) + w[4] * centre

    def prepare(lo, hi):
        def body(t, carry):
            k = 4.0 * raw[1, at(t), :]
            p, r = 2.0 * raw[2, at(t), :], 2.0 * raw[3, at(t), :]
            w = (k - p, k + p, k + r, k - r, 1.0 - 4.0 * k)
            for j in range(5):
                wts[j, at(t), :] = w[j]
            centre, above, below = trio(raw.at[0], t)
            moved = apply(centre, neighbours(centre, above, below), w)
            g_ref[at(t), :] = 0.25 * (moved - centre) + raw[4, at(t), :]
            return carry

        lax.fori_loop(lo, hi, body, 0)

    prepare(first + 1, last - 1)

    for side in range(2):
        edge = (0, pad + rows)[side]

        @pl.when(has[side])
        def _():
            remote(side, side).wait_recv()
            for a in range(5):
                raw[a, pl.ds(edge, pad), :] = recv[side, a].astype(jnp.float32)

        @pl.when(jnp.logical_not(has[side]))
        def _():
            for a in range(5):
                raw[a, pl.ds(edge, pad), :] = jnp.zeros((pad, cols), jnp.float32)

    low = (pad - halo + 1) // TILE
    high = -((-(pad + rows + halo - 1)) // TILE)
    prepare(low, first + 1)
    prepare(last - 1, high)

    def coefficient(j):
        value = jnp.float32(table[0][j])
        for n in range(1, len(table)):
            value = jnp.where(turn == n, jnp.float32(table[n][j]), value)
        return value

    def step(source, scale, target, q, lo, hi):
        def body(t, carry):
            centre, above, below = trio(source, t)
            around = neighbours(centre, above, below)
            w = [wts[j, at(t), :] for j in range(5)]
            value = apply(centre, around, w)
            if scale is not None:
                value = scale * value
            value = value + q * g_ref[at(t), :]
            if target is None:
                here = pl.ds(pl.multiple_of((t - first) * TILE, TILE), TILE)
                out_ref[0, here, :] = raw[0, at(t), :] + value
            else:
                target[at(t), :] = value
            return carry

        lax.fori_loop(lo, hi, body, 0)

    for m in range(degree):
        reach = degree - 1 - m
        lo = (pad - reach) // TILE
        hi = -((-(pad + rows + reach)) // TILE)
        source = g_ref if m == 0 else y_ref.at[(m - 1) % 2]
        scale = coefficient(degree) if m == 0 else None
        target = None if m == degree - 1 else y_ref.at[m % 2]
        step(source, scale, target, coefficient(degree - 1 - m), lo, hi)

    for side in range(2):
        @pl.when(has[side])
        def _():
            remote(side, 1 - side).wait_send()


def per_device(table, blocks, *args):
    rows, cols = args[0].shape
    halo = len(table[0])
    pad = -(-halo // 16) * 16
    ext = rows + 2 * pad
    f32, bf16 = jnp.float32, jnp.bfloat16
    return pl.pallas_call(
        functools.partial(kernel, table, halo, pad, blocks),
        out_shape=jax.ShapeDtypeStruct((1, rows, cols), f32),
        in_specs=[pl.BlockSpec(memory_space=pl.ANY)] * 5,
        out_specs=pl.BlockSpec(memory_space=pltpu.VMEM),
        scratch_shapes=[
            pltpu.VMEM((5, ext, cols), f32),
            pltpu.VMEM((5, ext, cols), f32),
            pltpu.VMEM((ext, cols), f32),
            pltpu.VMEM((2, ext, cols), f32),
            pltpu.VMEM((2, 5, pad, cols), bf16),
            pltpu.VMEM((2, 5, pad, cols), bf16),
            pltpu.SemaphoreType.DMA((5,)),
            pltpu.SemaphoreType.DMA((2,)),
            pltpu.SemaphoreType.DMA((2,)),
        ],
        compiler_params=pltpu.CompilerParams(
            collective_id=0, has_side_effects=True, vmem_limit_bytes=48 * 1024 * 1024
        ),
    )(*args)


def solution(mesh):
    table = end_polynomials(mesh.shape["tm"])
    spec = P(("ens", "space"), None)
    return jax.shard_map(
        functools.partial(per_device, table, mesh.shape["space"]),
        mesh=mesh,
        in_specs=(spec,) * 5,
        out_specs=P("tm", ("ens", "space"), None),
        check_vma=False,
    )
```

time: 146 us -> 24.2 us (0.17); the launches traced: 144 us -> 23.8 us
  starting transfers between devices: 61 us -> 0 us
  waiting for transfers between devices: 39.1 us -> 0 us
  other arithmetic: 25.9 us -> 0 us
  Pallas kernels: 0 us -> 17.8 us
  local copies, waits for them, and re-layouts: 17.2 us -> 6 us
    ppermute x18 -> x0, starting transfers between devices: 61 us -> none  [the longest x6 25.2 us: from_behind(): return lax.ppermute(value, axis, pairs)]
    ppermute x18 -> x0, waiting for transfers between devices: 39.1 us -> none  [the longest x6 36.7 us: from_behind(): return lax.ppermute(value, axis, pairs)]
    pallas_call x0 -> x1, Pallas kernels: none -> 17.8 us  [per_device(): pl.pallas_call(functools.partial(kernel, table, halo, pad, blocks), out_s...]
    convert_element_type x21 -> x0, other arithmetic: 10.6 us -> none  [the longest x6 6.18 us: advance(): ((coarse_step(padded, coefs_ext) + delta_wide) * row_mask).astype(jnp.bfl...]
    while x30 -> x0, local copies, waits for them, and re-layouts: 6.63 us -> none
    slice x34 -> x0, local copies, waits for them, and re-layouts: 5.82 us -> none  [the longest x28 4.62 us: tendency(): east_col = jnp.roll(centre, -1, axis=1)]
    mul x14 -> x0, other arithmetic: 4.14 us -> none  [the longest x4 2.12 us: fine_prop(): fine_step(padded, fine_wide[0], fine_wide[1], fine_wide[2], fine_wide[3])]
    unnamed x4 -> x0, other arithmetic: 3.16 us -> none
  transfers between devices with their start and end apart: 18 -> 0, of which waited for: 9 -> 0; matrix products, arithmetic and copies ran while one was open for 6% -> 0% of each run, Pallas kernels for 0% -> 0%
where the time goes in v1:
time: 24.2 us; the launch traced here: 23.8 us
  Pallas kernels  17.8 us (74%)
  local copies, waits for them, and re-layouts  6 us (25%)
    pallas_call x1, Pallas kernels, per_device(): pl.pallas_call(functools.partial(kernel, table, halo, pad, blocks), out_s...  17.8 us
    unnamed x11, local copies, waits for them, and re-layouts  6 us

profile of v1, /device:TPU:1, one launch (start us, length us, event | category | flops | bytes accessed | tf_op | source)
XLA Modules:
  0.0 23.8 jit_solution(14932609010429702979)
XLA Ops:
  0.0 0.0 copy-start
  0.0 1.0 %copy-done = f32[64,2048]{1,0:T(8,128)S(1)} copy-done((f32[64,2048]{1,0:T(8,128)S(1)}, f32[64,2048]{1,0:T(8,128)}, u32[]{:S(2)}) %copy-start) | copy-done | bytes 524312
  1.0 0.0 copy-start.1
  1.0 1.0 %copy-done.1 = f32[64,2048]{1,0:T(8,128)S(1)} copy-done((f32[64,2048]{1,0:T(8,128)S(1)}, f32[64,2048]{1,0:T(8,128)}, u32[]{:S(2)}) %copy-start.1) | copy-done | bytes 524312
  2.1 0.0 copy-start.2
  2.1 1.0 %copy-done.2 = f32[64,2048]{1,0:T(8,128)S(1)} copy-done((f32[64,2048]{1,0:T(8,128)S(1)}, f32[64,2048]{1,0:T(8,128)}, u32[]{:S(2)}) %copy-start.2) | copy-done | bytes 524312
  3.1 0.0 copy-start.3
  3.1 1.0 %copy-done.3 = f32[64,2048]{1,0:T(8,128)S(1)} copy-done((f32[64,2048]{1,0:T(8,128)S(1)}, f32[64,2048]{1,0:T(8,128)}, u32[]{:S(2)}) %copy-start.3) | copy-done | bytes 524312
  4.2 0.0 copy-start.4
  4.2 1.0 %copy-done.4 = f32[64,2048]{1,0:T(8,128)S(1)} copy-done((f32[64,2048]{1,0:T(8,128)S(1)}, f32[64,2048]{1,0:T(8,128)}, u32[]{:S(2)}) %copy-start.4) | copy-done | bytes 524312
  5.2 17.8 %shard_map.55 = f32[1,64,2048]{2,1,0:T(8,128)S(1)} custom-call(f32[64,2048]{1,0:T(8,128)S(1)} %copy-done, f32[64,2048]{1,0:T(8,128)S(1)} %copy-done.1, f32[64,2048]{1,0:T(8,128)S(1)} %copy-done.2, f32[64,2048]{1,0:T(8,128)S(1)} %copy-done.3, f32[64,2048]{1,0:T(8,128)S(1)} %copy-done.4), custom_call_target="tpu_custom_call" | custom-call | tf_op jit(solution)/shard_map/pallas_call | solution.py:208
  23.0 0.8 %copy.7 = f32[1,64,2048]{2,1,0:T(8,128)} copy(f32[1,64,2048]{2,1,0:T(8,128)S(1)} %shard_map.55) | data formatting | bytes 1048576
Async XLA Ops:
  0.0 1.0 %copy-start = (f32[64,2048]{1,0:T(8,128)S(1)}, f32[64,2048]{1,0:T(8,128)}, u32[]{:S(2)}) copy-start(f32[64,2048]{1,0:T(8,128)} %refs_0_.1) | copy-start | bytes 1572868
  1.0 1.0 %copy-start.1 = (f32[64,2048]{1,0:T(8,128)S(1)}, f32[64,2048]{1,0:T(8,128)}, u32[]{:S(2)}) copy-start(f32[64,2048]{1,0:T(8,128)} %refs_1_.1) | copy-start | bytes 1572868
  2.1 1.0 %copy-start.2 = (f32[64,2048]{1,0:T(8,128)S(1)}, f32[64,2048]{1,0:T(8,128)}, u32[]{:S(2)}) copy-start(f32[64,2048]{1,0:T(8,128)} %refs_2_.1) | copy-start | bytes 1572868
  3.1 1.0 %copy-start.3 = (f32[64,2048]{1,0:T(8,128)S(1)}, f32[64,2048]{1,0:T(8,128)}, u32[]{:S(2)}) copy-start(f32[64,2048]{1,0:T(8,128)} %refs_3_.1) | copy-start | bytes 1572868
  4.2 1.0 %copy-start.4 = (f32[64,2048]{1,0:T(8,128)S(1)}, f32[64,2048]{1,0:T(8,128)}, u32[]{:S(2)}) copy-start(f32[64,2048]{1,0:T(8,128)} %refs_4_.1) | copy-start | bytes 1572868

commit v2 on v1

--- a/solution.py
+++ b/solution.py
@@ -10,6 +10,8 @@
 
 FINE = 4
 TILE = 8
+UNROLL = 4
+STRAIGHT = 3
 MESH = pl.DeviceIdType.MESH
 
 
@@ -65,7 +67,23 @@
     return east, west, north, south
 
 
-def kernel(table, halo, pad, blocks, *refs):
+def over(lo, hi, body):
+    size = hi - lo
+    if size <= STRAIGHT:
+        for t in range(lo, hi):
+            body(t)
+        return
+    def several(i, carry):
+        for j in range(UNROLL):
+            body(lo + i * UNROLL + j)
+        return carry
+
+    lax.fori_loop(0, size // UNROLL, several, 0)
+    for t in range(hi - size % UNROLL, hi):
+        body(t)
+
+
+def kernel(table, halo, pad, blocks, overlap, *refs):
     args, out_ref = refs[:5], refs[5]
     raw, wts, g_ref, y_ref, send, recv, in_sem, send_sem, recv_sem = refs[6:]
     rows, cols = args[0].shape
@@ -112,13 +130,13 @@
             remote(side, 1 - side).start()
 
     def at(t):
-        return pl.ds(pl.multiple_of(t * TILE, TILE), TILE)
+        return pl.ds(t * TILE if isinstance(t, int) else pl.multiple_of(t * TILE, TILE), TILE)
 
     def trio(ref, t):
         return (
             ref[at(t), :],
-            ref[at(jnp.maximum(t - 1, 0)), :],
-            ref[at(jnp.minimum(t + 1, tiles - 1)), :],
+            ref[at(max(t - 1, 0) if isinstance(t, int) else jnp.maximum(t - 1, 0)), :],
+            ref[at(min(t + 1, tiles - 1) if isinstance(t, int) else jnp.minimum(t + 1, tiles - 1)), :],
         )
 
     def apply(centre, around, w):
@@ -126,7 +144,7 @@
         return (w[0] * east + w[1] * west) + (w[2] * north + w[3] * south) + w[4] * centre
 
     def prepare(lo, hi):
-        def body(t, carry):
+        def body(t):
             k = 4.0 * raw[1, at(t), :]
             p, r = 2.0 * raw[2, at(t), :], 2.0 * raw[3, at(t), :]
             w = (k - p, k + p, k + r, k - r, 1.0 - 4.0 * k)
@@ -135,39 +153,11 @@
             centre, above, below = trio(raw.at[0], t)
             moved = apply(centre, neighbours(centre, above, below), w)
             g_ref[at(t), :] = 0.25 * (moved - centre) + raw[4, at(t), :]
-            return carry
-
-        lax.fori_loop(lo, hi, body, 0)
-
-    prepare(first + 1, last - 1)
-
-    for side in range(2):
-        edge = (0, pad + rows)[side]
-
-        @pl.when(has[side])
-        def _():
-            remote(side, side).wait_recv()
-            for a in range(5):
-                raw[a, pl.ds(edge, pad), :] = recv[side, a].astype(jnp.float32)
-
-        @pl.when(jnp.logical_not(has[side]))
-        def _():
-            for a in range(5):
-                raw[a, pl.ds(edge, pad), :] = jnp.zeros((pad, cols), jnp.float32)
-
-    low = (pad - halo + 1) // TILE
-    high = -((-(pad + rows + halo - 1)) // TILE)
-    prepare(low, first + 1)
-    prepare(last - 1, high)
-
-    def coefficient(j):
-        value = jnp.float32(table[0][j])
-        for n in range(1, len(table)):
-            value = jnp.where(turn == n, jnp.float32(table[n][j]), value)
-        return value
+
+        over(lo, hi, body)
 
     def step(source, scale, target, q, lo, hi):
-        def body(t, carry):
+        def body(t):
             centre, above, below = trio(source, t)
             around = neighbours(centre, above, below)
             w = [wts[j, at(t), :] for j in range(5)]
@@ -176,22 +166,61 @@
                 value = scale * value
             value = value + q * g_ref[at(t), :]
             if target is None:
-                here = pl.ds(pl.multiple_of((t - first) * TILE, TILE), TILE)
+                here = at(t - first)
                 out_ref[0, here, :] = raw[0, at(t), :] + value
             else:
                 target[at(t), :] = value
-            return carry
-
-        lax.fori_loop(lo, hi, body, 0)
+
+        over(lo, hi, body)
+
+    def coefficient(j):
+        value = jnp.float32(table[0][j])
+        for n in range(1, len(table)):
+            value = jnp.where(turn == n, jnp.float32(table[n][j]), value)
+        return value
+
+    def advance(m, spans):
+        slots = y_ref.shape[0]
+        source = g_ref if m == 0 else y_ref.at[(m - 1) % slots]
+        scale = coefficient(degree) if m == 0 else None
+        target = None if m == degree - 1 else y_ref.at[m % slots]
+        q = coefficient(degree - 1 - m)
+        for lo, hi in spans:
+            step(source, scale, target, q, lo, hi)
+
+    prepare(first, last)
+    if overlap:
+        for m in range(degree):
+            advance(m, [(first, last)])
+
+    for side in range(2):
+        edge = (0, pad + rows)[side]
+
+        @pl.when(has[side])
+        def _():
+            remote(side, side).wait_recv()
+            for a in range(5):
+                raw[a, pl.ds(edge, pad), :] = recv[side, a].astype(jnp.float32)
+
+        @pl.when(jnp.logical_not(has[side]))
+        def _():
+            for a in range(5):
+                raw[a, pl.ds(edge, pad), :] = jnp.zeros((pad, cols), jnp.float32)
+
+    low = (pad - halo + 1) // TILE
+    high = -((-(pad + rows + halo - 1)) // TILE)
+    prepare(low, first + 1)
+    prepare(last - 1, high)
 
     for m in range(degree):
         reach = degree - 1 - m
         lo = (pad - reach) // TILE
         hi = -((-(pad + rows + reach)) // TILE)
-        source = g_ref if m == 0 else y_ref.at[(m - 1) % 2]
-        scale = coefficient(degree) if m == 0 else None
-        target = None if m == degree - 1 else y_ref.at[m % 2]
-        step(source, scale, target, coefficient(degree - 1 - m), lo, hi)
+        if overlap:
+            inner = -(-(pad + m + 2) // TILE)
+            advance(m, [(lo, inner), (first + last - inner, hi)])
+        else:
+            advance(m, [(lo, hi)])
 
     for side in range(2):
         @pl.when(has[side])
@@ -204,9 +233,10 @@
     halo = len(table[0])
     pad = -(-halo // 16) * 16
     ext = rows + 2 * pad
+    overlap = halo <= 12 and rows >= 4 * TILE
     f32, bf16 = jnp.float32, jnp.bfloat16
     return pl.pallas_call(
-        functools.partial(kernel, table, halo, pad, blocks),
+        functools.partial(kernel, table, halo, pad, blocks, overlap),
         out_shape=jax.ShapeDtypeStruct((1, rows, cols), f32),
         in_specs=[pl.BlockSpec(memory_space=pl.ANY)] * 5,
         out_specs=pl.BlockSpec(memory_space=pltpu.VMEM),
@@ -214,7 +244,7 @@
             pltpu.VMEM((5, ext, cols), f32),
             pltpu.VMEM((5, ext, cols), f32),
             pltpu.VMEM((ext, cols), f32),
-            pltpu.VMEM((2, ext, cols), f32),
+            pltpu.VMEM((halo - 2 if overlap else 2, ext, cols), f32),
             pltpu.VMEM((2, 5, pad, cols), bf16),
             pltpu.VMEM((2, 5, pad, cols), bf16),
             pltpu.SemaphoreType.DMA((5,)),
@@ -222,7 +252,7 @@
             pltpu.SemaphoreType.DMA((2,)),
         ],
         compiler_params=pltpu.CompilerParams(
-            collective_id=0, has_side_effects=True, vmem_limit_bytes=48 * 1024 * 1024
+            collective_id=0, has_side_effects=True, vmem_limit_bytes=63 * 1024 * 1024
         ),
     )(*args)
 

time: 24.2 us -> 15.3 us (0.63)
  Pallas kernels: 17.8 us -> 13.2 us
  local copies, waits for them, and re-layouts: 6 us -> 1.87 us
    pallas_call x1, Pallas kernels: 17.8 us -> 13.2 us  [per_device(): pl.pallas_call(functools.partial(kernel, table, halo, pad, blocks, overla...]
    unnamed x11 -> x1, local copies, waits for them, and re-layouts: 6 us -> 1.87 us
where the time goes in v2:
time: 15.3 us; the launch traced here: 15.1 us
  Pallas kernels  13.2 us (86%)
  local copies, waits for them, and re-layouts  1.87 us (12%)
    pallas_call x1, Pallas kernels, per_device(): pl.pallas_call(functools.partial(kernel, table, halo, pad, blocks, overla...  13.2 us
    unnamed x1, local copies, waits for them, and re-layouts  1.87 us

profile of v2, /device:TPU:1, one launch (start us, length us, event | category | flops | bytes accessed | tf_op | source)
XLA Modules:
  0.0 15.1 jit_solution(495448419607677630)
XLA Ops:
  0.0 13.2 %shard_map.55 = f32[1,64,2048]{2,1,0:T(8,128)} custom-call(f32[64,2048]{1,0:T(8,128)} %refs_0_.1, f32[64,2048]{1,0:T(8,128)} %refs_1_.1, f32[64,2048]{1,0:T(8,128)} %refs_2_.1, f32[64,2048]{1,0:T(8,128)} %refs_3_.1, f32[64,2048]{1,0:T(8,128)} %refs_4_.1), custom_call_target="tpu_custom_call" | custom-call | tf_op jit(solution)/shard_map/pallas_call | solution.py:238
  13.2 1.9 %copy.7 = f32[1,64,2048]{2,1,0:T(8,128)} copy(f32[1,64,2048]{2,1,0:T(8,128)} %shard_map.55) | data formatting | bytes 1048576

commit v3 on v2

--- a/solution.py
+++ b/solution.py
@@ -10,8 +10,8 @@
 
 FINE = 4
 TILE = 8
-UNROLL = 4
-STRAIGHT = 3
+UNROLL = 8
+STRAIGHT = 8
 MESH = pl.DeviceIdType.MESH
 
 
@@ -85,7 +85,7 @@
 
 def kernel(table, halo, pad, blocks, overlap, *refs):
     args, out_ref = refs[:5], refs[5]
-    raw, wts, g_ref, y_ref, send, recv, in_sem, send_sem, recv_sem = refs[6:]
+    raw, wts, g_ref, y_ref, pack, send, recv, in_sem, send_sem, recv_sem = refs[6:]
     rows, cols = args[0].shape
     tiles = (rows + 2 * pad) // TILE
     first, last = pad // TILE, (pad + rows) // TILE
@@ -94,12 +94,20 @@
     has = (me > 0, me < blocks - 1)
     peer = (me - 1, me + 1)
 
+    pieces = ((0, pad), (rows - pad, pad), (pad, rows - 2 * pad))
     loads = [
-        pltpu.make_async_copy(args[a], raw.at[a, pl.ds(pad, rows)], in_sem.at[a])
-        for a in range(5)
+        [
+            pltpu.make_async_copy(
+                args[a].at[pl.ds(r, size)], raw.at[a, pl.ds(pad + r, size)], in_sem.at[a, piece]
+            )
+            for a in range(5)
+        ]
+        for piece, (r, size) in enumerate(pieces)
+        if size > 0
     ]
-    for load in loads:
-        load.start()
+    for piece in loads:
+        for load in piece:
+            load.start()
     barrier = pltpu.get_barrier_semaphore()
     for side in range(2):
         @pl.when(has[side])
@@ -118,10 +126,24 @@
             device_id_type=MESH,
         )
 
+    near = halo // TILE * TILE
+    far = [(0, 5 * near, halo - near)]
+    for a in range(1, 5):
+        far.append((a, far[-1][1] + far[-1][2], max(halo - near - 1, 0)))
+    far = [entry for entry in far if entry[2] > 0]
+    spare = send.shape[1] - 5 * near
+    if spare > 0:
+        for side in range(2):
+            pack[side, pl.ds(5 * near, spare), :] = jnp.zeros((spare, cols), jnp.float32)
     for a in range(5):
-        loads[a].wait()
-        send[0, a] = raw[a, pl.ds(pad, pad), :].astype(jnp.bfloat16)
-        send[1, a] = raw[a, pl.ds(rows, pad), :].astype(jnp.bfloat16)
+        loads[0][a].wait()
+        loads[1][a].wait()
+        pack[0, pl.ds(a * near, near), :] = raw[a, pl.ds(pad, near), :]
+        pack[1, pl.ds(a * near, near), :] = raw[a, pl.ds(pad + rows - near, near), :]
+    for a, place, count in far:
+        pack[0, pl.ds(place, count), :] = raw[a, pl.ds(pad + near, count), :]
+        pack[1, pl.ds(place, count), :] = raw[a, pl.ds(pad + rows - near - count, count), :]
+    send[...] = pack[...].astype(jnp.bfloat16)
     peers = has[0].astype(jnp.int32) + has[1].astype(jnp.int32)
     pl.semaphore_wait(barrier, peers)
     for side in range(2):
@@ -188,10 +210,16 @@
         for lo, hi in spans:
             step(source, scale, target, q, lo, hi)
 
+    for piece in loads[2:]:
+        for load in piece:
+            load.wait()
+
     prepare(first, last)
     if overlap:
+        redone = -(-(degree + 1) // TILE)
         for m in range(degree):
-            advance(m, [(first, last)])
+            skip = max(0, redone - (degree - 1 - m))
+            advance(m, [(first + skip, last - skip)])
 
     for side in range(2):
         edge = (0, pad + rows)[side]
@@ -199,8 +227,13 @@
         @pl.when(has[side])
         def _():
             remote(side, side).wait_recv()
+            pack[side] = recv[side].astype(jnp.float32)
+            beside = (pad - near, pad + rows)[side]
             for a in range(5):
-                raw[a, pl.ds(edge, pad), :] = recv[side, a].astype(jnp.float32)
+                raw[a, pl.ds(beside, near), :] = pack[side, pl.ds(a * near, near), :]
+            for a, place, count in far:
+                away = (pad - near - count, pad + rows + near)[side]
+                raw[a, pl.ds(away, count), :] = pack[side, pl.ds(place, count), :]
 
         @pl.when(jnp.logical_not(has[side]))
         def _():
@@ -234,6 +267,8 @@
     pad = -(-halo // 16) * 16
     ext = rows + 2 * pad
     overlap = halo <= 12 and rows >= 4 * TILE
+    far = halo % TILE
+    packed = -(-(5 * (halo - far) + 5 * far - min(far, 1) * 4) // 16) * 16
     f32, bf16 = jnp.float32, jnp.bfloat16
     return pl.pallas_call(
         functools.partial(kernel, table, halo, pad, blocks, overlap),
@@ -245,9 +280,10 @@
             pltpu.VMEM((5, ext, cols), f32),
             pltpu.VMEM((ext, cols), f32),
             pltpu.VMEM((halo - 2 if overlap else 2, ext, cols), f32),
-            pltpu.VMEM((2, 5, pad, cols), bf16),
-            pltpu.VMEM((2, 5, pad, cols), bf16),
-            pltpu.SemaphoreType.DMA((5,)),
+            pltpu.VMEM((2, packed, cols), f32),
+            pltpu.VMEM((2, packed, cols), bf16),
+            pltpu.VMEM((2, packed, cols), bf16),
+            pltpu.SemaphoreType.DMA((5, 3)),
             pltpu.SemaphoreType.DMA((2,)),
             pltpu.SemaphoreType.DMA((2,)),
         ],

time: 15.3 us -> 12.7 us (0.83)
  Pallas kernels: 13.2 us -> 10.7 us
    pallas_call x1, Pallas kernels: 13.2 us -> 10.7 us  [per_device(): pl.pallas_call(functools.partial(kernel, table, halo, pad, blocks, overla...]
where the time goes in v3:
time: 12.7 us; the launch traced here: 12.5 us
  Pallas kernels  10.7 us (84%)
  local copies, waits for them, and re-layouts  1.87 us (15%)
    pallas_call x1, Pallas kernels, per_device(): pl.pallas_call(functools.partial(kernel, table, halo, pad, blocks, overla...  10.7 us
    unnamed x1, local copies, waits for them, and re-layouts  1.87 us

profile of v3, /device:TPU:1, one launch (start us, length us, event | category | flops | bytes accessed | tf_op | source)
XLA Modules:
  0.0 12.5 jit_solution(4878369876261733343)
XLA Ops:
  0.0 10.7 %shard_map.55 = f32[1,64,2048]{2,1,0:T(8,128)} custom-call(f32[64,2048]{1,0:T(8,128)} %refs_0_.1, f32[64,2048]{1,0:T(8,128)} %refs_1_.1, f32[64,2048]{1,0:T(8,128)} %refs_2_.1, f32[64,2048]{1,0:T(8,128)} %refs_3_.1, f32[64,2048]{1,0:T(8,128)} %refs_4_.1), custom_call_target="tpu_custom_call" | custom-call | tf_op jit(solution)/shard_map/pallas_call | solution.py:273
  10.7 1.9 %copy.7 = f32[1,64,2048]{2,1,0:T(8,128)} copy(f32[1,64,2048]{2,1,0:T(8,128)} %shard_map.55) | data formatting | bytes 1048576
